TPU v7x, 256 devices: a whole 4x4x8 slice. The times are simulated.
256 devices in a mesh: gx: 8 (over x, core), gy: 32 (over y, z).
Axes of the slice: x: 4, y: 4, z: 8, core: 2. Of those that a mesh axis runs over, the one named last changes fastest.
Arguments:
- prompt: bfloat16 [512, 8192], P('gx'), may hold values from -6 to 6
- dec_in: bfloat16 [2, 256, 8192], P(None, 'gy', 'gx'), may hold values from -6 to 6
- gate_codes: bfloat16 [8192, 53248], P('gx', 'gy'), may hold values from -127 to 127, as said below
- gate_scale: float32 [64, 53248], P('gx', 'gy'), may hold values from 5e-05 to 0.0005
- up_codes: bfloat16 [8192, 53248], P('gx', 'gy'), may hold values from -127 to 127, as said below
- up_scale: float32 [64, 53248], P('gx', 'gy'), may hold values from 5e-05 to 0.0005
- down_codes: bfloat16 [53248, 8192], P('gy', 'gx'), may hold values from -127 to 127, as said below
- down_scale: float32 [53248, 64], P('gy', 'gx'), may hold values from 2.5e-05 to 0.00025
Outputs:
- prompt_out: bfloat16 [512, 8192], P('gy', 'gx')
- dec_out: bfloat16 [2, 256, 8192], P(None, 'gy', 'gx')
Inputs may be any that keep to these rules, and one draw needn't show every extreme that they name: `gate_codes`: whole numbers. `up_codes`: whole numbers. `down_codes`: whole numbers.
All inputs are finite; a program needn't handle non-finite values.
Results may differ from a plain program's by a relative error of at most 0.034.
Values may be sent and summed in bfloat16 or wider, within the bound.
A program may use at most 192 MiB of HBM per device.

v0:
```python
import jax
import jax.numpy as jnp
from jax import lax
from jax.sharding import PartitionSpec as P


def dequant_rows(codes, scale):
    rows, cols = codes.shape
    full = codes.astype(jnp.float32).reshape(rows // 128, 128, cols) * scale[:, None, :]
    return full.reshape(rows, cols).astype(jnp.bfloat16)


def dequant_cols(codes, scale):
    rows, cols = codes.shape
    full = codes.astype(jnp.float32).reshape(rows, cols // 128, 128) * scale[:, :, None]
    return full.reshape(rows, cols).astype(jnp.bfloat16)


def swiglu(gate_up, hidden_width):
    return (jax.nn.silu(gate_up[:, :hidden_width]) * gate_up[:, hidden_width:]).astype(jnp.bfloat16)


def body(prompt, dec_in, gate_codes, gate_scale, up_codes, up_scale, down_codes, down_scale):
    hidden_width = gate_codes.shape[1]
    local_gate_up = jnp.concatenate(
        [dequant_rows(gate_codes, gate_scale), dequant_rows(up_codes, up_scale)], axis=1
    )
    down_weight = dequant_cols(down_codes, down_scale)

    def down_term(piece):
        return jnp.dot(piece, down_weight, preferred_element_type=jnp.float32)

    columns = lax.all_to_all(prompt, "gx", split_axis=1, concat_axis=0, tiled=True)
    prompt_gate_up = lax.psum_scatter(
        jnp.dot(columns, local_gate_up, preferred_element_type=jnp.float32).astype(jnp.bfloat16),
        "gx",
        scatter_dimension=0,
        tiled=True,
    ).astype(jnp.float32)
    prompt_hidden = swiglu(prompt_gate_up, hidden_width)
    prompt_terms = down_term(lax.all_gather(prompt_hidden, "gx", axis=0, tiled=True))
    prompt_out = lax.psum_scatter(
        prompt_terms.astype(jnp.bfloat16), "gy", scatter_dimension=0, tiled=True
    )
    results = []
    for step in range(dec_in.shape[0]):
        gathered = lax.all_gather(dec_in[step], "gy", axis=0, tiled=True)
        dec_gate_up = lax.psum_scatter(
            jnp.dot(gathered, local_gate_up, preferred_element_type=jnp.float32).astype(
                jnp.bfloat16
            ),
            "gx",
            scatter_dimension=0,
            tiled=True,
        ).astype(jnp.float32)
        dec_hidden = swiglu(dec_gate_up, hidden_width)
        dec_terms = down_term(lax.all_gather(dec_hidden, "gx", axis=0, tiled=True))
        results.append(
            lax.psum_scatter(dec_terms.astype(jnp.bfloat16), "gy", scatter_dimension=0, tiled=True)
        )
    dec_out = jnp.stack(results, axis=0)
    return (prompt_out, dec_out)


def solution(mesh):
    in_specs = (
        P("gx", None),
        P(None, "gy", "gx"),
        P("gx", "gy"),
        P("gx", "gy"),
        P("gx", "gy"),
        P("gx", "gy"),
        P("gy", "gx"),
        P("gy", "gx"),
    )
    out_specs = (P("gy", "gx"), P(None, "gy", "gx"))
    return jax.shard_map(body, mesh=mesh, in_specs=in_specs, out_specs=out_specs, check_vma=False)
```

profile of v0, /device:TPU:96, one launch (start us, length us, event | category | flops | bytes accessed | tf_op | source)
XLA Modules:
  0.0 874.6 jit_solution(2578851821156660151)
XLA Ops:
  7.2 2.5 copy.34
  9.7 4.3 all-to-all-start
  14.0 0.0 reduce-scatter.19.cloned.1.call-start
  14.0 6.2 fusion.1
  20.3 9.8 %all-to-all-done = bf16[64,8,1024]{2,0,1:T(8,128)(2,1)} async-done(((bf16[64,8,1024]{2,0,1:T(8,128)(2,1)}), bf16[64,8,1024]{2,0,1:T(8,128)(2,1)}, u32[]{:S(2)}, u32[]{:S(2)}) %all-to-all-start) | async-done | bytes 1048608 | tf_op jit(solution)/shard_map/all_to_all | solution.py:33
  30.0 7.0 fusion.3
  37.0 3.7 copy.24
  40.7 0.0 reduce-scatter.19.cloned.1.call-update
  40.7 0.0 reduce-scatter.21.cloned.1.call-start
  40.8 50.5 %all-gather = bf16[1,256,1024]{2,1,0:T(8,128)(2,1)S(1)} all-gather(bf16[1,8,1024]{2,1,0:T(8,128)(2,1)S(1)} %get-tuple-element.2), channel_id=2, replica_groups=mesh['gx'=8,'gy'=32] {'gy'}, dimensions={1}, use_global_device_ids=true | all-gather | bytes 540672 | tf_op jit(solution)/shard_map/all_gather | solution.py:47
  91.3 5.2 fusion.4
  96.5 3.8 copy.26
  100.3 0.0 reduce-scatter.21.cloned.1.call-update
  100.3 0.0 reduce-scatter.23.cloned.1.call-start
  100.4 48.5 %all-gather.1 = bf16[1,256,1024]{2,1,0:T(8,128)(2,1)S(1)} all-gather(bf16[1,8,1024]{2,1,0:T(8,128)(2,1)S(1)} %get-tuple-element.3), channel_id=3, replica_groups=mesh['gx'=8,'gy'=32] {'gy'}, dimensions={1}, use_global_device_ids=true | all-gather | bytes 540672 | tf_op jit(solution)/shard_map/all_gather | solution.py:47
  148.9 5.2 fusion.5
  154.1 3.8 copy.28
  157.9 0.0 reduce-scatter.23.cloned.1.call-update
  157.9 0.0 all-gather.4.cloned.1.call-start
  158.0 0.0 reduce-scatter.19.cloned.1.call-done
  158.0 1.1 convert_element_type.69
  159.1 0.8 fusion.8
  159.9 0.0 all-gather.4.cloned.1.call-update
  159.9 0.0 reduce-scatter.15.cloned.1.call-start
  160.0 0.3 copy.21
  160.3 1.9 mul.61
  162.2 0.0 copy-done.2
  162.2 2.3 fusion
  164.6 0.0 reduce-scatter.21.cloned.1.call-done
  164.6 1.0 convert_element_type.76
  165.6 0.1 fusion.10
  165.7 14.2 %all_gather.17 = bf16[256,1664]{1,0:T(8,128)(2,1)S(1)} all-gather(bf16[32,1664]{1,0:T(8,128)(2,1)S(1)} %fusion.10), channel_id=1, replica_groups=mesh['gx'=8,'gy'=32] {'gx'}, dimensions={0}, use_global_device_ids=true | all-gather | bytes 958464 | tf_op jit(solution)/shard_map/all_gather | solution.py:57
  179.9 2.0 convolution_convert_fusion.5
  181.8 0.0 reduce-scatter.15.cloned.1.call-update
  181.9 0.0 reduce-scatter.17.cloned.1.call-start
  181.9 8.6 reduce-scatter.23.cloned.1.call-done
  190.6 1.0 convert_element_type.81
  191.5 0.1 fusion.9
  191.6 13.5 %all_gather.19 = bf16[256,1664]{1,0:T(8,128)(2,1)S(1)} all-gather(bf16[32,1664]{1,0:T(8,128)(2,1)S(1)} %fusion.9), channel_id=1, replica_groups=mesh['gx'=8,'gy'=32] {'gx'}, dimensions={0}, use_global_device_ids=true | all-gather | bytes 958464 | tf_op jit(solution)/shard_map/all_gather | solution.py:57
  205.0 2.0 convolution_convert_fusion.4
  207.0 0.0 reduce-scatter.17.cloned.1.call-update
  207.0 0.0 reduce-scatter.13.cloned.1.call-start
  207.1 12.2 %all-gather.4.cloned.1.call-done = bf16[512,1664]{1,0:T(8,128)(2,1)} async-done(((bf16[64,1664]{1,0:T(8,128)(2,1)}), bf16[512,1664]{1,0:T(8,128)(2,1)}) %all-gather.4.cloned.1.call-update) | async-done | bytes 1703952 | tf_op jit(solution)/shard_map/all_gather | solution.py:41
  219.3 4.5 convolution_convert_fusion.3
  223.8 211.2 %reduce-scatter.15.cloned.1.call-done = bf16[8,1024]{1,0:T(8,128)(2,1)} async-done(((bf16[256,1024]{1,0:T(8,128)(2,1)}), bf16[8,1024]{1,0:T(8,128)(2,1)}) %reduce-scatter.15.cloned.1.call-update) | async-done | bytes 16400 | tf_op jit(solution)/shard_map/reduce_scatter | solution.py:59
  435.0 215.5 %reduce-scatter.17.cloned.1.call-done = bf16[8,1024]{1,0:T(8,128)(2,1)} async-done(((bf16[256,1024]{1,0:T(8,128)(2,1)}), bf16[8,1024]{1,0:T(8,128)(2,1)}) %reduce-scatter.17.cloned.1.call-update) | async-done | bytes 16400 | tf_op jit(solution)/shard_map/reduce_scatter | solution.py:59
  650.5 1.4 pad_maximum_fusion.4
  651.9 215.9 %reduce-scatter.13.cloned.1.call-done = bf16[16,1024]{1,0:T(8,128)(2,1)} async-done(((bf16[512,1024]{1,0:T(8,128)(2,1)}), bf16[16,1024]{1,0:T(8,128)(2,1)}) %reduce-scatter.13.cloned.1.call-update) | async-done | bytes 32784 | tf_op jit(solution)/shard_map/reduce_scatter | solution.py:42
  (15 shorter events, 0.1 us)
Async XLA Ops:
  7.2 6.8 copy-start.3
  7.2 6.8 copy-start
  7.2 6.8 copy-start.4
  9.7 20.4 %all-to-all-start = ((bf16[64,8,1024]{2,0,1:T(8,128)(2,1)}), bf16[64,8,1024]{2,0,1:T(8,128)(2,1)}, u32[]{:S(2)}, u32[]{:S(2)}) async-start(bf16[64,8,1024]{2,0,1:T(8,128)(2,1)} %bitcast.43), calls=%async_computation | async-start | bytes 2097152 | tf_op jit(solution)/shard_map/all_to_all | solution.py:33
  14.0 144.1 %reduce-scatter.19.cloned.1.call-start = ((), (), s32[]{:S(2)}) async-start(), calls=%async_computation.11 | async-start | bytes 3833856 | tf_op jit(solution)/shard_map/reduce_scatter | solution.py:34
  37.0 3.8 copy-start.6
  40.7 50.6 %copy-start.1 = (bf16[1024,1664]{1,0:T(8,128)(2,1)S(1)}, bf16[1024,1664]{1,0:T(8,128)(2,1)}, u32[]{:S(2)}) copy-start(bf16[1024,1664]{1,0:T(8,128)(2,1)} %get-tuple-element.4) | copy-start | bytes 10223620
  40.7 123.9 %reduce-scatter.21.cloned.1.call-start = ((), (), s32[]{:S(2)}) async-start(), calls=%async_computation.12 | async-start | bytes 1916928 | tf_op jit(solution)/shard_map/reduce_scatter | solution.py:48
  100.3 90.2 %reduce-scatter.23.cloned.1.call-start = ((), (), s32[]{:S(2)}) async-start(), calls=%async_computation.13 | async-start | bytes 1916928 | tf_op jit(solution)/shard_map/reduce_scatter | solution.py:48
  154.1 5.9 copy-start.5
  157.9 61.3 %all-gather.4.cloned.1.call-start = ((), (), s32[]{:S(2)}) async-start(), calls=%async_computation.7 | async-start | bytes 1916928 | tf_op jit(solution)/shard_map/all_gather | solution.py:41
  159.9 275.1 %reduce-scatter.15.cloned.1.call-start = ((), (), s32[]{:S(2)}) async-start(), calls=%async_computation.9 | async-start | bytes 540672 | tf_op jit(solution)/shard_map/reduce_scatter | solution.py:59
  160.3 2.0 copy-start.2
  181.9 468.7 %reduce-scatter.17.cloned.1.call-start = ((), (), s32[]{:S(2)}) async-start(), calls=%async_computation.10 | async-start | bytes 540672 | tf_op jit(solution)/shard_map/reduce_scatter | solution.py:59
  207.0 660.7 %reduce-scatter.13.cloned.1.call-start = ((), (), s32[]{:S(2)}) async-start(), calls=%async_computation.8 | async-start | bytes 1081344 | tf_op jit(solution)/shard_map/reduce_scatter | solution.py:42
Sparse Core Ops, SparseCore 0:
  40.9 38.7 reduce-scatter.18
  100.5 33.1 reduce-scatter.20
  158.1 32.4 reduce-scatter.22
  192.2 26.9 all-gather.3
  222.9 212.0 reduce-scatter.14
  439.1 211.3 reduce-scatter.16
  654.9 212.7 reduce-scatter.12
where the time goes:
time: 878 us; the launch traced here: 875 us
  waiting for transfers between devices  673 us (77%)
  blocking collectives  127 us (14%)
  matrix products  25.9 us (3%)
  local copies, waits for them, and re-layouts  16 us (2%)
  between operations  14.3 us (2%)
  other arithmetic  13.8 us (2%)
    reduce_scatter x2, waiting for transfers between devices, body(): lax.psum_scatter(dec_terms.astype(jnp.bfloat16), 'gy', scatter_dimension=...  427 us
    reduce_scatter x1, waiting for transfers between devices, body(): lax.psum_scatter(prompt_terms.astype(jnp.bfloat16), 'gy', scatter_dimensi...  216 us
    all_gather x2, blocking collectives, body(): gathered = lax.all_gather(dec_in[step], 'gy', axis=0, tiled=True)  98.9 us
    all_gather x2, blocking collectives, body(): dec_terms = down_term(lax.all_gather(dec_hidden, 'gx', axis=0, tiled=True))  27.7 us
  transfers between devices with their start and end apart: 8, of which 6 were waited for; matrix products, arithmetic and copies ran while one was open for 5% of the time, Pallas kernels for 0%

commit v1 on v0

v1 whole, which is shorter than its diff:
```python
import jax
import jax.numpy as jnp
from jax import lax
from jax.experimental import pallas as pl
from jax.experimental.pallas import tpu as pltpu
from jax.sharding import PartitionSpec as P

MESH = pl.DeviceIdType.MESH
NX, NC, NY, NZ = 4, 2, 4, 8
BF, F32 = jnp.bfloat16, jnp.float32
ROWS = 256
CHUNKS = 4
GROUP = 16
PIECE = ROWS // (NX * NC)
HALF = ROWS // 2


def kernel(
    prompt, dec, gate, gate_scale, up, up_scale, down, down_scale,
    prompt_out, dec_out,
    w, sc, wd, ds, x_buf, dec_buf, p_buf, px_buf, q_buf, m1_buf, m2_buf, h_buf, o_buf, ry_buf, sy_buf, rz_buf,
    load_sem, own_sem, pr_send, pr_recv, dy_send, dy_recv, dz_send, dz_recv,
    ex_send, ex_recv, q_send, m1_recv, m2_recv, a_send, a_recv, c_send, c_recv, y_send, y_recv, z_send, z_recv,
):
    gx, gy = lax.axis_index("gx"), lax.axis_index("gy")
    x, c = gx // NC, lax.rem(gx, NC)
    y, z = gy // NZ, lax.rem(gy, NZ)
    width, ff = gate.shape
    half_of_z = lax.rem(z // 2, 2)
    slot_of_z = (z // 4) * 2 + lax.rem(z, 2)

    def at_gx(m):
        return (lax.rem(gx + m, NX * NC), gy)

    def at_x(m):
        return (lax.rem(x + m + NX, NX) * NC + c, gy)

    def at_y(m):
        return (gx, lax.rem(y + m, NY) * NZ + z)

    def at_z(m):
        return (gx, y * NZ + lax.rem(z + m, NZ))

    partner = (x * NC + 1 - c, gy)
    side = (at_x(-1), at_x(1))
    chip = (lax.rem(x + NX - 1, NX), lax.rem(x + 1, NX))
    across = lax.rem(x + 2, NX)

    def remote(src, dst, send, recv, where):
        return pltpu.make_async_remote_copy(
            src_ref=src, dst_ref=dst, send_sem=send, recv_sem=recv, device_id=where, device_id_type=MESH
        )

    loads = [
        pltpu.make_async_copy(gate, w.at[:, pl.ds(0, ff)], load_sem.at[0]),
        pltpu.make_async_copy(gate_scale, sc.at[:, pl.ds(0, ff)], load_sem.at[1]),
        pltpu.make_async_copy(up, w.at[:, pl.ds(ff, ff)], load_sem.at[2]),
        pltpu.make_async_copy(up_scale, sc.at[:, pl.ds(ff, ff)], load_sem.at[3]),
        pltpu.make_async_copy(dec, dec_buf, load_sem.at[4]),
        pltpu.make_async_copy(down, wd, load_sem.at[5]),
        pltpu.make_async_copy(down_scale, ds, load_sem.at[6]),
    ]
    loads[4].start()
    for i in (0, 1, 2, 3, 5, 6):
        loads[i].start()

    barrier = pltpu.get_barrier_semaphore()
    peers = [at_gx(m) for m in range(1, 8)] + [at_y(m) for m in range(1, 4)] + [at_z(m) for m in range(1, 8)]
    for peer in peers:
        pl.semaphore_signal(barrier, inc=1, device_id=peer, device_id_type=MESH)

    loads[4].wait()
    dec_rows = pl.ds(pl.multiple_of(slot_of_z * GROUP, GROUP), GROUP)
    x_buf[2 + half_of_z, y, dec_rows, :] = jnp.concatenate([dec_buf[0], dec_buf[1]], axis=0)
    pl.semaphore_wait(barrier, len(peers))

    prompt_rows = pl.ds(pl.multiple_of(c * 2 * GROUP, 2 * GROUP), 2 * GROUP)
    prompt_copies = []
    own_copies = []
    for h in range(2):
        src_rows = pl.ds(h * 2 * GROUP, 2 * GROUP)
        place = x_buf.at[h, x, prompt_rows, :]
        own = pltpu.make_async_copy(
            prompt.at[src_rows, pl.ds(pl.multiple_of(gx * width, width), width)], place, own_sem.at[h]
        )
        own.start()
        own_copies.append(own)
        group = []
        for m in range(1, 8):
            to = lax.rem(gx + m, NX * NC)
            copy = remote(
                prompt.at[src_rows, pl.ds(pl.multiple_of(to * width, width), width)],
                place, pr_send.at[h, m - 1], pr_recv.at[h, m - 1], at_gx(m),
            )
            copy.start()
            group.append(copy)
        prompt_copies.append(group)

    dec_block = x_buf.at[2 + half_of_z, y, dec_rows, :]
    dy_copies = []
    for m in range(1, 4):
        copy = remote(dec_block, dec_block, dy_send.at[m - 1], dy_recv.at[m - 1], at_y(m))
        copy.start()
        dy_copies.append(copy)

    def dequant_gate_up():
        for i in (0, 1, 2, 3):
            loads[i].wait()

        def tile(j, carry):
            cols = pl.ds(pl.multiple_of(j * 256, 256), 256)
            for r in range(8):
                rows = pl.ds(r * 128, 128)
                w[rows, cols] = (w[rows, cols].astype(F32) * sc[pl.ds(r, 1), cols]).astype(BF)
            return carry

        lax.fori_loop(0, 2 * ff // 256, tile, 0)

    def dequant_down():
        for i in (5, 6):
            loads[i].wait()

        def tile(j, carry):
            rows = pl.ds(pl.multiple_of(j * 128, 128), 128)
            for b in range(8):
                cols = pl.ds(b * 128, 128)
                wd[rows, cols] = (wd[rows, cols].astype(F32) * ds[rows, pl.ds(b, 1)]).astype(BF)
            return carry

        lax.fori_loop(0, ff // 128, tile, 0)

    dz_copies = []

    def decode_z():
        for copy in dy_copies:
            copy.wait_recv()
        column = x_buf.at[2 + half_of_z, :, dec_rows, :]
        for m in range(1, 8):
            copy = remote(column, column, dz_send.at[m - 1], dz_recv.at[m - 1], at_z(m))
            copy.start()
            dz_copies.append(copy)

    def wait_input(k):
        if k < 2:
            own_copies[k].wait()
            for copy in prompt_copies[k]:
                copy.wait_recv()
        elif k == 2:
            for copy in dz_copies:
                copy.wait_recv()

    theirs = pl.ds(pl.multiple_of((1 - c) * HALF, HALF), HALF)

    def exchange(k):
        return remote(p_buf.at[k, theirs, :], px_buf.at[k], ex_send.at[k], ex_recv.at[k], partner)

    def stage1(k):
        def tile(j, carry):
            cols = pl.ds(pl.multiple_of(j * 256, 256), 256)
            product = jnp.dot(x_buf[k].reshape(ROWS, width), w[:, cols], preferred_element_type=F32)
            p_buf[k, :, cols] = product.astype(BF)
            remote(
                p_buf.at[k, theirs, cols], px_buf.at[k, :, cols], ex_send.at[k], ex_recv.at[k], partner
            ).start()
            return carry

        lax.fori_loop(0, 2 * ff // 256, tile, 0)

    def own_rows(start):
        return pl.ds(pl.multiple_of(c * HALF + start, GROUP), GROUP)

    def px_rows(start):
        return pl.ds(pl.multiple_of(start, GROUP), GROUP)

    def pair_sum(k, start, cols):
        return p_buf[k, own_rows(start), cols].astype(F32) + px_buf[k, px_rows(start), cols].astype(F32)

    def columns(n, step, fn):
        def tile(j, carry):
            fn(pl.multiple_of(j * step, step))
            return carry

        lax.fori_loop(0, n // step, tile, 0)

    pending = []

    def q_copy(k, kind, d):
        src = q_buf.at[k, kind, d]
        if kind == 0:
            return remote(src, m1_buf.at[k, d], q_send.at[k, 0, d], m1_recv.at[k, d], side[d])
        half = 1 - d if kind == 1 else d
        return remote(
            src, m2_buf.at[k, d, pl.ds(half * GROUP, GROUP), :],
            q_send.at[k, kind, d], m2_recv.at[k, kind - 1, d], side[d],
        )

    def send(copy):
        copy.start()
        pending.append(copy)

    def stage2(k):
        exchange(k).wait_recv()
        for kind in (0, 1):
            starts = [(across * PIECE + d * GROUP) if kind == 0 else (chip[d] * PIECE + (1 - d) * GROUP) for d in (0, 1)]

            def fn(j):
                cols = pl.ds(j, 256)
                for d in (0, 1):
                    q_buf[k, kind, d, :, cols] = pair_sum(k, starts[d], cols).astype(BF)

            columns(2 * ff, 256, fn)
            for d in (0, 1):
                send(q_copy(k, kind, d))

    def stage3(k):
        for d in (0, 1):
            q_copy(k, 0, d).wait_recv()

        def fn(j):
            cols = pl.ds(j, 256)
            for d in (0, 1):
                total = pair_sum(k, chip[d] * PIECE + d * GROUP, cols) + m1_buf[k, d, :, cols].astype(F32)
                q_buf[k, 2, d, :, cols] = total.astype(BF)

        columns(2 * ff, 256, fn)
        for d in (0, 1):
            send(q_copy(k, 2, d))

    def piece_rows(core, at, start=0, size=PIECE):
        return pl.ds(pl.multiple_of(core * HALF + at * PIECE + start, GROUP), size)

    def a_copy(k, step, d):
        if step == 0:
            part = h_buf.at[k, piece_rows(c, x), :]
        else:
            part = h_buf.at[k, piece_rows(c, chip[1 - d], d * GROUP, GROUP), :]
        return remote(part, part, a_send.at[k, step, d], a_recv.at[k, step, d], side[d])

    def c_copy(k, i):
        at = (x, chip[0], chip[1], across)[i]
        part = h_buf.at[k, piece_rows(c, at), :]
        return remote(part, part, c_send.at[k, i], c_recv.at[k, i], partner)

    def stage4(k):
        for kind in (1, 2):
            for d in (0, 1):
                q_copy(k, kind, d).wait_recv()

        def fn(j):
            for r in (0, GROUP):
                values = []
                for first in (0, ff):
                    cols = pl.ds(pl.multiple_of(first + j, 128), 128)
                    total = pair_sum(k, x * PIECE + r, cols)
                    for d in (0, 1):
                        total = total + m2_buf[k, d, pl.ds(r, GROUP), cols].astype(F32)
                    values.append(total)
                g, u = values
                rows = pl.ds(pl.multiple_of(c * HALF + x * PIECE + r, GROUP), GROUP)
                h_buf[k, rows, pl.ds(j, 128)] = (g / (1.0 + jnp.exp(-g)) * u).astype(BF)

        columns(ff, 128, fn)
        for d in (0, 1):
            send(a_copy(k, 0, d))
        send(c_copy(k, 0))

    def stage5(k):
        for d in (0, 1):
            a_copy(k, 0, d).wait_recv()
        for d in (0, 1):
            send(a_copy(k, 1, d))
        send(c_copy(k, 1))
        send(c_copy(k, 2))

    def stage6(k):
        for d in (0, 1):
            a_copy(k, 1, d).wait_recv()
        send(c_copy(k, 3))

    def y_copy(k, m):
        return remote(
            o_buf.at[k, lax.rem(y + m, NY)], ry_buf.at[k, m - 1], y_send.at[k, m - 1], y_recv.at[k, m - 1], at_y(m)
        )

    def stage7(k):
        for i in range(4):
            c_copy(k, i).wait_recv()

        def tile(j, carry):
            cols = pl.ds(pl.multiple_of(j * 256, 256), 256)
            product = jnp.dot(h_buf[k], wd[:, cols], preferred_element_type=F32)
            o_buf[k, :, :, cols] = product.astype(BF).reshape(NY, ROWS // NY, 256)
            return carry

        lax.fori_loop(0, width // 256, tile, 0)
        for m in range(1, 4):
            send(y_copy(k, m))

    def z_copy(k, i):
        to = (i // 2) * 4 + (k % 2) * 2 + i % 2
        m = lax.rem(to - z + NZ, NZ)
        slot = lax.rem(m + NZ - 1, NZ)
        return to, remote(
            sy_buf.at[k, pl.ds(i * GROUP, GROUP), :], rz_buf.at[k // 2, slot],
            z_send.at[k, i], z_recv.at[k // 2, slot], (gx, y * NZ + to),
        )

    def stage8(k):
        for m in range(1, 4):
            y_copy(k, m).wait_recv()

        def fn(j):
            cols = pl.ds(j, 256)
            total = o_buf[k, y, :, cols].astype(F32)
            for m in range(3):
                total = total + ry_buf[k, m, :, cols].astype(F32)
            sy_buf[k, :, cols] = total.astype(BF)

        columns(width, 256, fn)
        for i in range(4):
            to, copy = z_copy(k, i)

            @pl.when(to != z)
            def _():
                copy.start()

    def stage9(kind):
        for m in range(NZ - 1):
            slot = rz_buf.at[kind, m]
            remote(slot, slot, z_send.at[0, 0], z_recv.at[kind, m], at_z(1)).wait_recv()
        rows = pl.ds(pl.multiple_of(slot_of_z * GROUP, GROUP), GROUP)
        k = kind * 2 + half_of_z
        for j in range(0, width, 256):
            cols = pl.ds(j, 256)
            total = sy_buf[k, rows, cols].astype(F32)
            for m in range(NZ - 1):
                total = total + rz_buf[kind, m, :, cols].astype(F32)
            total = total.astype(BF)
            if kind == 0:
                prompt_out[:, cols] = total
            else:
                dec_out[0, :, cols] = total[0:8]
                dec_out[1, :, cols] = total[8:16]

    dequant_gate_up()
    decode_z()
    wait_input(0)
    stage1(0)
    stage2(0)
    wait_input(1)
    stage1(1)
    dequant_down()
    stage3(0)
    stage2(1)
    stage4(0)
    wait_input(2)
    stage1(2)
    stage3(1)
    stage2(2)
    stage5(0)
    stage4(1)
    stage6(0)
    stage1(3)
    stage3(2)
    stage2(3)
    stage7(0)
    stage5(1)
    stage4(2)
    stage6(1)
    stage8(0)
    stage3(3)
    stage7(1)
    stage5(2)
    stage4(3)
    stage6(2)
    stage8(1)
    stage5(3)
    stage7(2)
    stage6(3)
    stage9(0)
    stage8(2)
    stage7(3)
    stage8(3)
    stage9(1)

    for group in prompt_copies:
        for copy in group:
            copy.wait_send()
    for copy in dy_copies + dz_copies + pending:
        copy.wait_send()
    for k in range(CHUNKS):
        exchange(k).wait_send()
        for i in range(4):
            to, copy = z_copy(k, i)

            @pl.when(to != z)
            def _():
                copy.wait_send()


def body(prompt, dec_in, gate_codes, gate_scale, up_codes, up_scale, down_codes, down_scale):
    width, ff = gate_codes.shape
    dma = pltpu.SemaphoreType.DMA
    any_spec = pl.BlockSpec(memory_space=pl.ANY)
    vmem = pl.BlockSpec(memory_space=pltpu.VMEM)
    return pl.pallas_call(
        kernel,
        out_shape=(
            jax.ShapeDtypeStruct((GROUP, width), BF),
            jax.ShapeDtypeStruct(dec_in.shape, BF),
        ),
        in_specs=[any_spec] * 8,
        out_specs=(vmem, vmem),
        scratch_shapes=[
            pltpu.VMEM((width, 2 * ff), BF),
            pltpu.VMEM((8, 2 * ff), F32),
            pltpu.VMEM((ff, width), BF),
            pltpu.VMEM((ff, 8), F32),
            pltpu.VMEM((CHUNKS, NY, ROWS // NY, width), BF),
            pltpu.VMEM(dec_in.shape, BF),
            pltpu.VMEM((CHUNKS, ROWS, 2 * ff), BF),
            pltpu.VMEM((CHUNKS, HALF, 2 * ff), BF),
            pltpu.VMEM((CHUNKS, 3, 2, GROUP, 2 * ff), BF),
            pltpu.VMEM((CHUNKS, 2, GROUP, 2 * ff), BF),
            pltpu.VMEM((CHUNKS, 2, PIECE, 2 * ff), BF),
            pltpu.VMEM((CHUNKS, ROWS, ff), BF),
            pltpu.VMEM((CHUNKS, NY, ROWS // NY, width), BF),
            pltpu.VMEM((CHUNKS, 3, ROWS // NY, width), BF),
            pltpu.VMEM((CHUNKS, ROWS // NY, width), BF),
            pltpu.VMEM((2, NZ - 1, GROUP, width), BF),
            dma((7,)),
            dma((2,)),
            dma((2, 7)),
            dma((2, 7)),
            dma((3,)),
            dma((3,)),
            dma((7,)),
            dma((7,)),
            dma((CHUNKS,)),
            dma((CHUNKS,)),
            dma((CHUNKS, 3, 2)),
            dma((CHUNKS, 2)),
            dma((CHUNKS, 2, 2)),
            dma((CHUNKS, 2, 2)),
            dma((CHUNKS, 2, 2)),
            dma((CHUNKS, 4)),
            dma((CHUNKS, 4)),
            dma((CHUNKS, 3)),
            dma((CHUNKS, 3)),
            dma((CHUNKS, 4)),
            dma((2, NZ - 1)),
        ],
        compiler_params=pltpu.CompilerParams(
            collective_id=0, has_side_effects=True, vmem_limit_bytes=60 * 1024 * 1024
        ),
        cost_estimate=pl.CostEstimate(flops=10_500_000_000, bytes_accessed=12_000_000, transcendentals=1_000_000),
        name="ffn",
    )(prompt, dec_in, gate_codes, gate_scale, up_codes, up_scale, down_codes, down_scale)


def solution(mesh):
    in_specs = (
        P("gx", None),
        P(None, "gy", "gx"),
        P("gx", "gy"),
        P("gx", "gy"),
        P("gx", "gy"),
        P("gx", "gy"),
        P("gy", "gx"),
        P("gy", "gx"),
    )
    out_specs = (P("gy", "gx"), P(None, "gy", "gx"))
    return jax.shard_map(body, mesh=mesh, in_specs=in_specs, out_specs=out_specs, check_vma=False)
```

time: 878 us -> 111 us (0.13)
  waiting for transfers between devices: 673 us -> 0 us
  blocking collectives: 127 us -> 0 us
  Pallas kernels: 0 us -> 103 us
  matrix products: 25.9 us -> 0 us
  other arithmetic: 13.8 us -> 0 us
  between operations: 14.3 us -> 0.64 us
  local copies, waits for them, and re-layouts: 16 us -> 4.77 us
    reduce_scatter x6 -> x0, waiting for transfers between devices: 651 us -> none  [the longest x2 427 us: body(): lax.psum_scatter(dec_terms.astype(jnp.bfloat16), 'gy', scatter_dimension=...]
    all_gather x4 -> x0, blocking collectives: 127 us -> none  [the longest x2 98.9 us: body(): gathered = lax.all_gather(dec_in[step], 'gy', axis=0, tiled=True)]
    pallas_call x0 -> x1, Pallas kernels: none -> 103 us  [body(): pl.pallas_call(kernel, out_shape=(jax.ShapeDtypeStruct((GROUP, width), BF...]
    dot_general x6 -> x0, matrix products: 25.9 us -> none  [the longest x2 10.5 us: body(): jnp.dot(gathered, local_gate_up, preferred_element_type=jnp.float32)]
    convert_element_type x8 -> x0, other arithmetic: 12.5 us -> none  [the longest x1 6.24 us: dequant_rows(): return full.reshape(rows, cols).astype(jnp.bfloat16)]
    all_gather x1 -> x0, waiting for transfers between devices: 12.2 us -> none  [body(): lax.all_gather(prompt_hidden, 'gx', axis=0, tiled=True)]
    all_to_all x1 -> x0, waiting for transfers between devices: 9.76 us -> none  [body(): lax.all_to_all(prompt, 'gx', split_axis=1, concat_axis=0, tiled=True)]
  transfers between devices with their start and end apart: 8 -> 0, of which waited for: 6 -> 0; matrix products, arithmetic and copies ran while one was open for 5% -> 0% of each run, Pallas kernels for 0% -> 0%
where the time goes in v1:
time: 111 us; the launch traced here: 109 us
  Pallas kernels  103 us (93%)
  local copies, waits for them, and re-layouts  4.77 us (4%)
    pallas_call x1, Pallas kernels, body(): pl.pallas_call(kernel, out_shape=(jax.ShapeDtypeStruct((GROUP, width), BF...  103 us
    unnamed x3, local copies, waits for them, and re-layouts  4.77 us

profile of v1, /device:TPU:96, one launch (start us, length us, event | category | flops | bytes accessed | tf_op | source)
XLA Modules:
  0.0 108.9 jit_solution(15913229427451751767)
XLA Ops:
  0.6 2.0 %copy.10.down_scale = f32[1664,8]{1,0:T(8,128)} copy(f32[1664,8]{0,1:T(8,128)} %param.15) | data formatting | bytes 106496 | tf_op args[7]
  2.6 103.5 %ffn.1 = (bf16[16,1024]{1,0:T(8,128)(2,1)}, bf16[2,8,1024]{2,1,0:T(8,128)(2,1)}) custom-call(bf16[64,8192]{1,0:T(8,128)(2,1)} %prompt.1, bf16[2,8,1024]{2,1,0:T(8,128)(2,1)} %dec.1, bf16[1024,1664]{1,0:T(8,128)(2,1)} %gate.1, f32[8,1664]{1,0:T(8,128)} %gate_scale.1, bf16[1024,1664]{1,0:T(8,128)(2,1)} %up.1, f32[8,1664]{1,0:T(8,128)} %up_scale.1, ...), custom_call_target="tpu_custom_call" | custom-call | flops 10499999744 | bytes 12000000 | tf_op jit(solution)/shard_map/ffn/pallas_call | solution.py:406
  106.1 1.4 %copy.13 = bf16[16,1024]{1,0:T(8,128)(2,1)} copy(bf16[16,1024]{1,0:T(8,128)(2,1)} %get-tuple-element.4) | data formatting | bytes 65536
  107.5 1.4 %copy.14 = bf16[2,8,1024]{2,1,0:T(8,128)(2,1)} copy(bf16[2,8,1024]{2,1,0:T(8,128)(2,1)} %get-tuple-element.5) | data formatting | bytes 65536

commit v2 on v0

v2 whole, which is shorter than its diff:
```python
import jax
import jax.numpy as jnp
from jax import lax
from jax.experimental import pallas as pl
from jax.experimental.pallas import tpu as pltpu
from jax.sharding import PartitionSpec as P

MESH = pl.DeviceIdType.MESH
NX, NC, NY, NZ = 4, 2, 4, 8
BF, F32 = jnp.bfloat16, jnp.float32
GROUP = 16
NQ = 4
ROWS = NY * 2 * GROUP
CHUNKS = 2 * NQ
PIECE = ROWS // (NX * NC)
HALF = ROWS // 2
DIRECT = 2
DEQ = 4

OFFSETS = (0, 0.5, 1.65, 3.1, 4.4, 5.8, 6.2, 8.7)


def stage_order():
    steps = [(k + at, -i, i, k) for k in range(CHUNKS) for i, at in enumerate(OFFSETS)]
    return [(i, k) for _, _, i, k in sorted(steps)]


def kernel(
    prompt, dec, gate, gate_scale, up, up_scale, down, down_scale,
    prompt_out, dec_out,
    w, sc, wd, ds, x_buf, pb_buf, dec_buf, p_buf, px_buf, q_buf, m1_buf, m2_buf, h_buf, o_buf, ry_buf, sy_buf, rz_buf,
    load_sem, down_sem, dec_sem, own_sem, pc_send, pc_recv, px_send, px_recv, py_send, py_recv, dz_send, dz_recv, dy_send, dy_recv,
    ex_send, ex_recv, q_send, m1_recv, m2_recv, a_send, a_recv, c_send, c_recv, y_send, y_recv, z_send, z_recv,
):
    gx, gy = lax.axis_index("gx"), lax.axis_index("gy")
    x, c = gx // NC, lax.rem(gx, NC)
    y, z = gy // NZ, lax.rem(gy, NZ)
    width, ff = gate.shape
    my_q, my_zh = lax.rem(z, NQ), z // NQ

    def chip_at(m):
        return lax.rem(x + m, NX)

    def at_x(m):
        return (chip_at(m) * NC + c, gy)

    def at_y(m):
        return (gx, lax.rem(y + m, NY) * NZ + z)

    def at_z(m):
        return (gx, y * NZ + lax.rem(z + m, NZ))

    partner = (x * NC + 1 - c, gy)
    side = (at_x(NX - 1), at_x(1))
    chip = (chip_at(NX - 1), chip_at(1))
    across = chip_at(2)

    def remote(src, dst, send, recv, where):
        return pltpu.make_async_remote_copy(
            src_ref=src, dst_ref=dst, send_sem=send, recv_sem=recv, device_id=where, device_id_type=MESH
        )

    pending = []

    def send(copy):
        copy.start()
        pending.append(copy)

    dec_load = pltpu.make_async_copy(dec, dec_buf, dec_sem.at[0])
    dec_load.start()
    part = width // DEQ
    loads = []
    for i in range(DEQ):
        rows, scales = pl.ds(i * part, part), pl.ds(i * part // 128, part // 128)
        if i == 0:
            loads.append([
                pltpu.make_async_copy(gate_scale, sc.at[:, pl.ds(0, ff)], load_sem.at[DEQ, 0]),
                pltpu.make_async_copy(up_scale, sc.at[:, pl.ds(ff, ff)], load_sem.at[DEQ, 1]),
            ])
        else:
            loads.append([])
        loads[i].append(pltpu.make_async_copy(gate.at[rows, :], w.at[rows, pl.ds(0, ff)], load_sem.at[i, 0]))
        loads[i].append(pltpu.make_async_copy(up.at[rows, :], w.at[rows, pl.ds(ff, ff)], load_sem.at[i, 1]))
        for load in loads[i]:
            load.start()
    down_loads = [
        pltpu.make_async_copy(down, wd, down_sem.at[0]),
        pltpu.make_async_copy(down_scale, ds, down_sem.at[1]),
    ]
    for load in down_loads:
        load.start()

    barrier = pltpu.get_barrier_semaphore()
    peers = [partner] + [at_x(m) for m in range(1, NX)]
    peers += [at_y(m) for m in range(1, NY)] + [at_z(m) for m in range(1, NZ)]
    for peer in peers:
        pl.semaphore_signal(barrier, inc=1, device_id=peer, device_id_type=MESH)

    dec_load.wait()
    x_buf[1, my_q, y, my_zh] = jnp.concatenate([dec_buf[0], dec_buf[1]], axis=0)
    pl.semaphore_wait(barrier, len(peers))

    share = width // NY

    def prompt_cols(q):
        if q < DIRECT:
            return pl.ds(0, width)
        return pl.ds(pl.multiple_of(y * share, share), share)

    def prompt_part(q, m, core):
        size = width if q < DIRECT else share
        first = (chip_at(m) * NC + core) * width + (0 if q < DIRECT else y * share)
        return prompt.at[q, :, pl.ds(pl.multiple_of(first, share), size)]

    def prompt_place(q, core):
        return x_buf.at[0, q, x, core, :, prompt_cols(q)]

    def prompt_core(q, m):
        dst = prompt_place(q, c) if m == 0 else pb_buf.at[q, m - 1, :, prompt_cols(q)]
        return remote(prompt_part(q, m, 1 - c), dst, pc_send.at[q, m], pc_recv.at[q, m], partner)

    def prompt_x(q, m, core):
        src = prompt_part(q, m, c) if core == 0 else pb_buf.at[q, m - 1, :, prompt_cols(q)]
        dst = prompt_place(q, c if core == 0 else 1 - c)
        return remote(src, dst, px_send.at[q, m - 1, core], px_recv.at[q, m - 1, core], at_x(m))

    def prompt_own(q):
        return pltpu.make_async_copy(prompt_part(q, 0, c), prompt_place(q, c), own_sem.at[q])

    def prompt_y(q, m):
        block = x_buf.at[0, q, :, :, :, prompt_cols(q)]
        return remote(block, block, py_send.at[q, m - 1], py_recv.at[q, m - 1], at_y(m))

    def prompt_start(q):
        prompt_own(q).start()
        for m in (2, 1, 3):
            send(prompt_x(q, m, 0))

    def prompt_forward(q):
        for m in (2, 1, 3):
            prompt_core(q, m).wait_recv()
            send(prompt_x(q, m, 1))

    def prompt_along_x(q):
        prompt_own(q).wait()
        prompt_core(q, 0).wait_recv()
        for m in (1, 3, 2):
            for core in (0, 1):
                prompt_x(q, m, core).wait_recv()

    def prompt_along_y(q):
        prompt_along_x(q)
        for m in (2, 1, 3):
            send(prompt_y(q, m))

    dec_block = x_buf.at[1, my_q, y, my_zh]
    for q in range(NQ):
        for m in (2, 1, 3, 0):
            send(prompt_core(q, m))
        if q == 0:
            prompt_start(0)
            for m in (4, 3, 5, 2, 6, 1, 7):
                send(remote(dec_block, dec_block, dz_send.at[m - 1], dz_recv.at[z], at_z(m)))
    prompt_forward(0)
    for q in range(DIRECT, NQ):
        prompt_start(q)
        prompt_forward(q)
    for q in range(1, DIRECT):
        prompt_start(q)
        prompt_forward(q)

    def decode_y(q):
        for zh in (0, 1):
            block = x_buf.at[1, q, y, zh]

            @pl.when(z != zh * NQ + q)
            def _():
                remote(block, block, dz_send.at[0], dz_recv.at[zh * NQ + q], at_z(1)).wait_recv()

        for m in (1, 3, 2):
            send(decode_y_copy(q, m))

    def decode_y_copy(q, m):
        block = x_buf.at[1, q, y]
        return remote(block, block, dy_send.at[q, m - 1], dy_recv.at[q, m - 1], at_y(m))

    def wait_input(k):
        if k < DIRECT:
            prompt_along_x(k)
        elif k < NQ:
            for m in (1, 3, 2):
                prompt_y(k, m).wait_recv()
        else:
            for m in (1, 3, 2):
                decode_y_copy(k - NQ, m).wait_recv()

    def dequant_gate_up(i):
        for load in loads[i]:
            load.wait()

        def tile(j, carry):
            cols = pl.ds(pl.multiple_of(j * 256, 256), 256)
            for r in range(i * part // 128, (i + 1) * part // 128):
                rows = pl.ds(r * 128, 128)
                w[rows, cols] = (w[rows, cols].astype(F32) * sc[pl.ds(r, 1), cols]).astype(BF)
            return carry

        lax.fori_loop(0, 2 * ff // 256, tile, 0)

    def dequant_down():
        for load in down_loads:
            load.wait()

        def tile(j, carry):
            rows = pl.ds(pl.multiple_of(j * 128, 128), 128)
            scales = ds[:, rows].T
            for b in range(8):
                cols = pl.ds(b * 128, 128)
                wd[rows, cols] = (wd[rows, cols].astype(F32) * scales[:, b : b + 1]).astype(BF)
            return carry

        lax.fori_loop(0, ff // 128, tile, 0)

    theirs = pl.ds(pl.multiple_of((1 - c) * HALF, HALF), HALF)
    sides = (pl.ds(0, ff), pl.ds(ff, ff))

    def exchange(k, s):
        return remote(
            p_buf.at[k, theirs, sides[s]], px_buf.at[k, :, sides[s]], ex_send.at[k, s], ex_recv.at[k, s], partner
        )

    def stage1(k):
        wait_input(k)
        rows = x_buf[k // NQ, k % NQ].reshape(ROWS, width)
        for s in (0, 1):
            p_buf[k, :, sides[s]] = jnp.dot(rows, w[:, sides[s]], preferred_element_type=F32).astype(BF)
            send(exchange(k, s))

    def pair_sum(k, at, s):
        own = pl.ds(pl.multiple_of(c * HALF + at * PIECE, PIECE), PIECE)
        got = pl.ds(pl.multiple_of(at * PIECE, PIECE), PIECE)
        return p_buf[k, own, sides[s]].astype(F32) + px_buf[k, got, sides[s]].astype(F32)

    def q_copy(k, kind, d):
        src = q_buf.at[k, kind, d]
        if kind == 0:
            return remote(src, m1_buf.at[k, d], q_send.at[k, 0, d], m1_recv.at[k, d], side[d])
        s = 1 - d if kind == 1 else d
        return remote(src, m2_buf.at[k, d, s], q_send.at[k, kind, d], m2_recv.at[k, kind - 1, d], side[d])

    def stage2(k):
        for s in (0, 1):
            exchange(k, s).wait_recv()
        for kind in (0, 1):
            for d in (0, 1):
                at, s = (across, d) if kind == 0 else (chip[d], 1 - d)
                q_buf[k, kind, d] = pair_sum(k, at, s).astype(BF)
                send(q_copy(k, kind, d))

    def stage3(k):
        for d in (0, 1):
            q_copy(k, 0, d).wait_recv()
            q_buf[k, 2, d] = (pair_sum(k, chip[d], d) + m1_buf[k, d].astype(F32)).astype(BF)
            send(q_copy(k, 2, d))

    def piece(k, core, at, cols=pl.ds(0, 1664)):
        return h_buf.at[k, pl.ds(pl.multiple_of(core * HALF + at * PIECE, PIECE), PIECE), cols]

    cut = ff // 256 * 128 + 128
    cuts = (pl.ds(0, cut), pl.ds(cut, ff - cut))

    def a_copy(k, step, d):
        block = piece(k, c, x) if step == 0 else piece(k, c, chip[1 - d], cuts[d])
        return remote(block, block, a_send.at[k, step, d], a_recv.at[k, step, d], side[d])

    def c_copy(k, i):
        block = piece(k, c, (x, chip[0], chip[1], across)[i])
        return remote(block, block, c_send.at[k, i], c_recv.at[k, i], partner)

    def stage4(k):
        for kind in (1, 2):
            for d in (0, 1):
                q_copy(k, kind, d).wait_recv()
        g, u = [
            pair_sum(k, x, s) + m2_buf[k, 0, s].astype(F32) + m2_buf[k, 1, s].astype(F32) for s in (0, 1)
        ]
        own = pl.ds(pl.multiple_of(c * HALF + x * PIECE, PIECE), PIECE)
        h_buf[k, own, :] = (g / (1.0 + jnp.exp(-g)) * u).astype(BF)
        for d in (0, 1):
            send(a_copy(k, 0, d))
        send(c_copy(k, 0))

    def stage5(k):
        for d in (0, 1):
            a_copy(k, 0, d).wait_recv()
            send(a_copy(k, 1, d))
        send(c_copy(k, 1))
        send(c_copy(k, 2))

    def stage6(k):
        for d in (0, 1):
            a_copy(k, 1, d).wait_recv()
        send(c_copy(k, 3))

    def y_copy(k, m):
        return remote(
            o_buf.at[k, lax.rem(y + m, NY)], ry_buf.at[k, m - 1], y_send.at[k, m - 1], y_recv.at[k, m - 1], at_y(m)
        )

    def stage7(k):
        for i in range(4):
            c_copy(k, i).wait_recv()
        product = jnp.dot(h_buf[k], wd[...], preferred_element_type=F32)
        o_buf[k] = product.astype(BF).reshape(NY, ROWS // NY, width)
        for m in (1, 3, 2):
            send(y_copy(k, m))

    def z_copy(k, zh):
        to = zh * NQ + k % NQ
        slot = lax.rem(to - z + 2 * NZ - 1, NZ)
        return to, remote(
            sy_buf.at[k, pl.ds(zh * GROUP, GROUP), :], rz_buf.at[k // NQ, slot],
            z_send.at[k, zh], z_recv.at[k // NQ, slot], (gx, y * NZ + to),
        )

    def stage8(k):
        for m in (1, 3, 2):
            y_copy(k, m).wait_recv()
        for j in range(0, width, 256):
            cols = pl.ds(j, 256)
            total = o_buf[k, y, :, cols].astype(F32)
            for m in range(3):
                total = total + ry_buf[k, m, :, cols].astype(F32)
            sy_buf[k, :, cols] = total.astype(BF)
        for zh in (0, 1):
            to, copy = z_copy(k, zh)

            @pl.when(to != z)
            def _():
                copy.start()

    def finish(kind):
        for m in range(NZ - 1):
            slot = rz_buf.at[kind, m]
            remote(slot, slot, z_send.at[0, 0], z_recv.at[kind, m], at_z(1)).wait_recv()
        rows = pl.ds(pl.multiple_of(my_zh * GROUP, GROUP), GROUP)
        for j in range(0, width, 256):
            cols = pl.ds(j, 256)
            total = sy_buf[kind * NQ + my_q, rows, cols].astype(F32)
            for m in range(NZ - 1):
                total = total + rz_buf[kind, m, :, cols].astype(F32)
            total = total.astype(BF)
            if kind == 0:
                prompt_out[:, cols] = total
            else:
                dec_out[0, :, cols] = total[0:8]
                dec_out[1, :, cols] = total[8:16]

    stages = (stage1, stage2, stage3, stage4, stage5, stage6, stage7, stage8)
    for i in range(DEQ):
        dequant_gate_up(i)
    for q in range(DIRECT, NQ):
        prompt_along_y(q)
    for i, k in stage_order():
        if (i, k) == (1, 0):
            for q in range(NQ):
                decode_y(q)
        if (i, k) == (1, 1):
            dequant_down()
        stages[i](k)
    finish(0)
    finish(1)

    for copy in pending:
        copy.wait_send()
    for k in range(CHUNKS):
        for zh in (0, 1):
            to, copy = z_copy(k, zh)

            @pl.when(to != z)
            def _():
                copy.wait_send()


def body(prompt, dec_in, gate_codes, gate_scale, up_codes, up_scale, down_codes, down_scale):
    width, ff = gate_codes.shape
    dma = pltpu.SemaphoreType.DMA
    any_spec = pl.BlockSpec(memory_space=pl.ANY)
    vmem = pl.BlockSpec(memory_space=pltpu.VMEM)
    return pl.pallas_call(
        kernel,
        out_shape=(
            jax.ShapeDtypeStruct((GROUP, width), BF),
            jax.ShapeDtypeStruct(dec_in.shape, BF),
        ),
        in_specs=[any_spec] * 8,
        out_specs=(vmem, vmem),
        scratch_shapes=[
            pltpu.VMEM((width, 2 * ff), BF),
            pltpu.VMEM((8, 2 * ff), F32),
            pltpu.VMEM((ff, width), BF),
            pltpu.VMEM((8, ff), F32),
            pltpu.VMEM((2, NQ, NY, 2, GROUP, width), BF),
            pltpu.VMEM((NQ, NX - 1, GROUP, width), BF),
            pltpu.VMEM(dec_in.shape, BF),
            pltpu.VMEM((CHUNKS, ROWS, 2 * ff), BF),
            pltpu.VMEM((CHUNKS, HALF, 2 * ff), BF),
            pltpu.VMEM((CHUNKS, 3, 2, PIECE, ff), BF),
            pltpu.VMEM((CHUNKS, 2, PIECE, ff), BF),
            pltpu.VMEM((CHUNKS, 2, 2, PIECE, ff), BF),
            pltpu.VMEM((CHUNKS, ROWS, ff), BF),
            pltpu.VMEM((CHUNKS, NY, ROWS // NY, width), BF),
            pltpu.VMEM((CHUNKS, 3, ROWS // NY, width), BF),
            pltpu.VMEM((CHUNKS, ROWS // NY, width), BF),
            pltpu.VMEM((2, NZ - 1, GROUP, width), BF),
            dma((DEQ + 1, 2)),
            dma((2,)),
            dma((1,)),
            dma((NQ,)),
            dma((NQ, NX)),
            dma((NQ, NX)),
            dma((NQ, NX - 1, 2)),
            dma((NQ, NX - 1, 2)),
            dma((NQ, NY - 1)),
            dma((NQ, NY - 1)),
            dma((NZ - 1,)),
            dma((NZ,)),
            dma((NQ, NY - 1)),
            dma((NQ, NY - 1)),
            dma((CHUNKS, 2)),
            dma((CHUNKS, 2)),
            dma((CHUNKS, 3, 2)),
            dma((CHUNKS, 2)),
            dma((CHUNKS, 2, 2)),
            dma((CHUNKS, 2, 2)),
            dma((CHUNKS, 2, 2)),
            dma((CHUNKS, 4)),
            dma((CHUNKS, 4)),
            dma((CHUNKS, 3)),
            dma((CHUNKS, 3)),
            dma((CHUNKS, 2)),
            dma((2, NZ - 1)),
        ],
        compiler_params=pltpu.CompilerParams(
            collective_id=0, has_side_effects=True, vmem_limit_bytes=60 * 1024 * 1024
        ),
        cost_estimate=pl.CostEstimate(flops=10_500_000_000, bytes_accessed=12_000_000, transcendentals=1_000_000),
        name="ffn",
    )(
        prompt.reshape(NQ, GROUP, prompt.shape[1]), dec_in, gate_codes, gate_scale, up_codes, up_scale, down_codes,
        down_scale.T,
    )


def solution(mesh):
    in_specs = (
        P("gx", None),
        P(None, "gy", "gx"),
        P("gx", "gy"),
        P("gx", "gy"),
        P("gx", "gy"),
        P("gx", "gy"),
        P("gy", "gx"),
        P("gy", "gx"),
    )
    out_specs = (P("gy", "gx"), P(None, "gy", "gx"))
    return jax.shard_map(body, mesh=mesh, in_specs=in_specs, out_specs=out_specs, check_vma=False)
```

time: 878 us -> 90.4 us (0.10)
  waiting for transfers between devices: 673 us -> 0 us
  blocking collectives: 127 us -> 0 us
  Pallas kernels: 0 us -> 86.8 us
  matrix products: 25.9 us -> 0 us
  other arithmetic: 13.8 us -> 0 us
  between operations: 14.3 us -> 0.64 us
  local copies, waits for them, and re-layouts: 16 us -> 2.75 us
    reduce_scatter x6 -> x0, waiting for transfers between devices: 651 us -> none  [the longest x2 427 us: body(): lax.psum_scatter(dec_terms.astype(jnp.bfloat16), 'gy', scatter_dimension=...]
    all_gather x4 -> x0, blocking collectives: 127 us -> none  [the longest x2 98.9 us: body(): gathered = lax.all_gather(dec_in[step], 'gy', axis=0, tiled=True)]
    pallas_call x0 -> x1, Pallas kernels: none -> 86.8 us  [body(): pl.pallas_call(kernel, out_shape=(jax.ShapeDtypeStruct((GROUP, width), BF...]
    dot_general x6 -> x0, matrix products: 25.9 us -> none  [the longest x2 10.5 us: body(): jnp.dot(gathered, local_gate_up, preferred_element_type=jnp.float32)]
    convert_element_type x8 -> x0, other arithmetic: 12.5 us -> none  [the longest x1 6.24 us: dequant_rows(): return full.reshape(rows, cols).astype(jnp.bfloat16)]
    all_gather x1 -> x0, waiting for transfers between devices: 12.2 us -> none  [body(): lax.all_gather(prompt_hidden, 'gx', axis=0, tiled=True)]
    all_to_all x1 -> x0, waiting for transfers between devices: 9.76 us -> none  [body(): lax.all_to_all(prompt, 'gx', split_axis=1, concat_axis=0, tiled=True)]
    unnamed x18 -> x2, local copies, waits for them, and re-layouts: 11.7 us -> 2.75 us
  transfers between devices with their start and end apart: 8 -> 0, of which waited for: 6 -> 0; matrix products, arithmetic and copies ran while one was open for 5% -> 0% of each run, Pallas kernels for 0% -> 0%
where the time goes in v2:
time: 90.4 us; the launch traced here: 90.2 us
  Pallas kernels  86.8 us (96%)
  local copies, waits for them, and re-layouts  2.75 us (3%)
    pallas_call x1, Pallas kernels, body(): pl.pallas_call(kernel, out_shape=(jax.ShapeDtypeStruct((GROUP, width), BF...  86.8 us
    unnamed x2, local copies, waits for them, and re-layouts  2.75 us

profile of v2, /device:TPU:96, one launch (start us, length us, event | category | flops | bytes accessed | tf_op | source)
XLA Modules:
  0.0 90.2 jit_solution(11634379997887503956)
XLA Ops:
  0.6 86.8 %ffn.1 = (bf16[16,1024]{1,0:T(8,128)(2,1)}, bf16[2,8,1024]{2,1,0:T(8,128)(2,1)}) custom-call(bf16[4,16,8192]{2,1,0:T(8,128)(2,1)} %bitcast.2, bf16[2,8,1024]{2,1,0:T(8,128)(2,1)} %dec.1, bf16[1024,1664]{1,0:T(8,128)(2,1)} %gate.1, f32[8,1664]{1,0:T(8,128)} %gate_scale.1, bf16[1024,1664]{1,0:T(8,128)(2,1)} %up.1, f32[8,1664]{1,0:T(8,128)} %up_scale.1, ...), custom_call_target="tpu_custom_call" | custom-call | flops 10499999744 | bytes 12000000 | tf_op jit(solution)/shard_map/ffn/pallas_call | solution.py:390
  87.5 1.4 %copy.12 = bf16[16,1024]{1,0:T(8,128)(2,1)} copy(bf16[16,1024]{1,0:T(8,128)(2,1)} %get-tuple-element.4) | data formatting | bytes 65536
  88.9 1.4 %copy.13 = bf16[2,8,1024]{2,1,0:T(8,128)(2,1)} copy(bf16[2,8,1024]{2,1,0:T(8,128)(2,1)} %get-tuple-element.5) | data formatting | bytes 65536

commit v3 on v2

--- a/solution.py
+++ b/solution.py
@@ -27,7 +27,7 @@
 
 def kernel(
     prompt, dec, gate, gate_scale, up, up_scale, down, down_scale,
-    prompt_out, dec_out,
+    out,
     w, sc, wd, ds, x_buf, pb_buf, dec_buf, p_buf, px_buf, q_buf, m1_buf, m2_buf, h_buf, o_buf, ry_buf, sy_buf, rz_buf,
     load_sem, down_sem, dec_sem, own_sem, pc_send, pc_recv, px_send, px_recv, py_send, py_recv, dz_send, dz_recv, dy_send, dy_recv,
     ex_send, ex_recv, q_send, m1_recv, m2_recv, a_send, a_recv, c_send, c_recv, y_send, y_recv, z_send, z_recv,
@@ -87,8 +87,6 @@
         pltpu.make_async_copy(down, wd, down_sem.at[0]),
         pltpu.make_async_copy(down_scale, ds, down_sem.at[1]),
     ]
-    for load in down_loads:
-        load.start()
 
     barrier = pltpu.get_barrier_semaphore()
     peers = [partner] + [at_x(m) for m in range(1, NX)]
@@ -251,11 +249,11 @@
     def stage2(k):
         for s in (0, 1):
             exchange(k, s).wait_recv()
-        for kind in (0, 1):
-            for d in (0, 1):
-                at, s = (across, d) if kind == 0 else (chip[d], 1 - d)
-                q_buf[k, kind, d] = pair_sum(k, at, s).astype(BF)
-                send(q_copy(k, kind, d))
+            q_buf[k, 0, s] = pair_sum(k, across, s).astype(BF)
+            send(q_copy(k, 0, s))
+        for s in (0, 1):
+            q_buf[k, 1, 1 - s] = pair_sum(k, chip[1 - s], s).astype(BF)
+            send(q_copy(k, 1, 1 - s))
 
     def stage3(k):
         for d in (0, 1):
@@ -350,15 +348,14 @@
             for m in range(NZ - 1):
                 total = total + rz_buf[kind, m, :, cols].astype(F32)
             total = total.astype(BF)
-            if kind == 0:
-                prompt_out[:, cols] = total
-            else:
-                dec_out[0, :, cols] = total[0:8]
-                dec_out[1, :, cols] = total[8:16]
+            out[kind, :, cols] = total
 
     stages = (stage1, stage2, stage3, stage4, stage5, stage6, stage7, stage8)
     for i in range(DEQ):
         dequant_gate_up(i)
+        if i == DEQ - 2:
+            for load in down_loads:
+                load.start()
     for q in range(DIRECT, NQ):
         prompt_along_y(q)
     for i, k in stage_order():
@@ -382,19 +379,22 @@
                 copy.wait_send()
 
 
+def split_kernel(both, prompt_out, dec_out):
+    prompt_out[...] = both[0]
+    dec_out[0] = both[1, 0:8]
+    dec_out[1] = both[1, 8:16]
+
+
 def body(prompt, dec_in, gate_codes, gate_scale, up_codes, up_scale, down_codes, down_scale):
     width, ff = gate_codes.shape
     dma = pltpu.SemaphoreType.DMA
     any_spec = pl.BlockSpec(memory_space=pl.ANY)
     vmem = pl.BlockSpec(memory_space=pltpu.VMEM)
-    return pl.pallas_call(
+    both = pl.pallas_call(
         kernel,
-        out_shape=(
-            jax.ShapeDtypeStruct((GROUP, width), BF),
-            jax.ShapeDtypeStruct(dec_in.shape, BF),
-        ),
+        out_shape=jax.ShapeDtypeStruct((2, GROUP, width), BF),
         in_specs=[any_spec] * 8,
-        out_specs=(vmem, vmem),
+        out_specs=vmem,
         scratch_shapes=[
             pltpu.VMEM((width, 2 * ff), BF),
             pltpu.VMEM((8, 2 * ff), F32),
@@ -450,6 +450,16 @@
         prompt.reshape(NQ, GROUP, prompt.shape[1]), dec_in, gate_codes, gate_scale, up_codes, up_scale, down_codes,
         down_scale.T,
     )
+    return pl.pallas_call(
+        split_kernel,
+        out_shape=(
+            jax.ShapeDtypeStruct((GROUP, width), BF),
+            jax.ShapeDtypeStruct(dec_in.shape, BF),
+        ),
+        in_specs=[vmem],
+        out_specs=(vmem, vmem),
+        name="split",
+    )(both)
 
 
 def solution(mesh):

time: 90.4 us -> 88 us (0.973)
  local copies, waits for them, and re-layouts: 2.75 us -> 0 us
    unnamed x2 -> x0, local copies, waits for them, and re-layouts: 2.75 us -> none
    pallas_call x1 -> x2, Pallas kernels: 86.8 us -> 87.2 us  [the longest x1 85.7 us: body(): pl.pallas_call(kernel, out_shape=jax.ShapeDtypeStruct((2, GROUP, width),...]
where the time goes in v3:
time: 88 us; the launch traced here: 87.8 us
  Pallas kernels  87.2 us (99%)
    pallas_call x1, Pallas kernels, body(): pl.pallas_call(kernel, out_shape=jax.ShapeDtypeStruct((2, GROUP, width),...  85.7 us

profile of v3, /device:TPU:96, one launch (start us, length us, event | category | flops | bytes accessed | tf_op | source)
XLA Modules:
  0.0 87.8 jit_solution(13566442504330281389)
XLA Ops:
  0.6 85.7 %ffn.1.both = bf16[2,16,1024]{2,1,0:T(8,128)(2,1)} custom-call(bf16[4,16,8192]{2,1,0:T(8,128)(2,1)} %bitcast.2, bf16[2,8,1024]{2,1,0:T(8,128)(2,1)} %dec.1, bf16[1024,1664]{1,0:T(8,128)(2,1)} %gate.1, f32[8,1664]{1,0:T(8,128)} %gate_scale.1, bf16[1024,1664]{1,0:T(8,128)(2,1)} %up.1, f32[8,1664]{1,0:T(8,128)} %up_scale.1, bf16[1664,1024]{1,0:T(8,128)(2,1)} %down.1, ...), custom_call_target="tpu_custom_call" | custom-call | flops 10499999744 | bytes 12000000 | tf_op jit(solution)/shard_map/ffn/pallas_call | solution.py:393
  86.4 1.5 %split.1 = (bf16[16,1024]{1,0:T(8,128)(2,1)}, bf16[2,8,1024]{2,1,0:T(8,128)(2,1)}) custom-call(bf16[2,16,1024]{2,1,0:T(8,128)(2,1)} %ffn.1.both), custom_call_target="tpu_custom_call" | custom-call | tf_op jit(solution)/shard_map/split/pallas_call | solution.py:453
